TPU v7x, 512 devices: a whole 4x8x8 slice. The times are simulated.
512 devices in a mesh: xy: 32 (over z_hi, y), gz: 16 (over x, z_lo, core).
Axes of the slice: x: 4, y: 8, z: 8 (z_hi: 4, z_lo: 2; z = z_hi * 2 + z_lo), core: 2. Of those that a mesh axis runs over, the one named last changes fastest.
Arguments:
- volume: float32 [64, 1024, 2048], P('gz', 'xy'), may hold values from -6 to 6
- measured: float32 [4, 1024, 2048], P(None, 'xy'), may hold values from -6 to 6
- ray_offset: int32 [4, 64], replicated, may hold values from -128 to 127, as said below
- defocus: int32 [4, 16], replicated, may hold values from 8000 to 39999
Outputs:
- updated: float32 [64, 1024, 2048], P('gz', 'xy')
Inputs may be any that keep to these rules, and one draw needn't show every extreme that they name: `ray_offset`: one tilt has offset -128 at the first layer and 127 at the last.
All inputs are finite; a program needn't handle non-finite values.
Results may differ from a plain program's by a relative error of at most 0.0003.
Values sent between devices are 32-bit elements; how exact they have to be, the bound alone decides.
A program may use at most 64 MiB of HBM per device.

v0:
```python
import math

import jax
import jax.numpy as jnp
from jax import lax
from jax.sharding import PartitionSpec as P

HALO = 16


pixel_size = 4.0
wavelength = 0.0197
contrast = 0.07
amplitude_root = math.sqrt(1.0 - 0.07 * 0.07)
highest = lax.Precision.HIGHEST


def extended(cells, sides, width):
    for axis, dim in sides:
        count = lax.axis_size(axis)
        ends = count - 1
        head = lax.slice_in_dim(cells, 0, width, axis=dim)
        tail = lax.slice_in_dim(cells, cells.shape[dim] - width, cells.shape[dim], axis=dim)
        cells = jnp.concatenate(
            [
                lax.ppermute(tail, axis, [(i, (i + 1) % count) for i in range(ends)]),
                cells,
                lax.ppermute(head, axis, [((i + 1) % count, i) for i in range(ends)]),
            ],
            axis=dim,
        )
    return cells


def turn_table(first_len, second_len, period):
    first_idx = lax.broadcasted_iota(jnp.int32, (first_len, second_len), 0)
    second_idx = lax.broadcasted_iota(jnp.int32, (first_len, second_len), 1)
    angle = 2.0 * math.pi / period * (first_idx * second_idx % period).astype(jnp.float32)
    return (jnp.cos(angle), jnp.sin(angle))


def ctf_response(defocus, length):
    small_len = length // 128
    low_idx = lax.broadcasted_iota(jnp.int32, (small_len, 128), 0)
    high_idx = lax.broadcasted_iota(jnp.int32, (small_len, 128), 1)
    freq_index = low_idx + small_len * high_idx
    frequency = jnp.where(2 * freq_index < length, freq_index, freq_index - length).astype(
        jnp.float32
    ) / (length * pixel_size)
    phase = (
        math.pi * wavelength * defocus.astype(jnp.float32)[:, :, None, None] * frequency * frequency
    )
    return -(amplitude_root * jnp.sin(phase) + contrast * jnp.cos(phase))


def ctf_filter(lines, response):
    length = lines.shape[-1]
    small_len = length // 128
    cos_small, sin_small = turn_table(small_len, small_len, small_len)
    cos_large, sin_large = turn_table(128, 128, 128)
    twist_cos, twist_sin = turn_table(small_len, 128, length)
    split = lines.reshape(lines.shape[:-1] + (small_len, 128))
    first_re = jnp.einsum("...ab,ak->...kb", split, cos_small, precision=highest)
    first_im = -jnp.einsum("...ab,ak->...kb", split, sin_small, precision=highest)
    turned_re = first_re * twist_cos + first_im * twist_sin
    turned_im = first_im * twist_cos - first_re * twist_sin
    spec_re = jnp.matmul(turned_re, cos_large, precision=highest) + jnp.matmul(
        turned_im, sin_large, precision=highest
    )
    spec_im = jnp.matmul(turned_im, cos_large, precision=highest) - jnp.matmul(
        turned_re, sin_large, precision=highest
    )
    spec_re = spec_re * response
    spec_im = spec_im * response
    back_re = jnp.matmul(spec_re, cos_large, precision=highest) - jnp.matmul(
        spec_im, sin_large, precision=highest
    )
    back_im = jnp.matmul(spec_im, cos_large, precision=highest) + jnp.matmul(
        spec_re, sin_large, precision=highest
    )
    untwist_re = back_re * twist_cos - back_im * twist_sin
    untwist_im = back_im * twist_cos + back_re * twist_sin
    result = jnp.einsum("...kb,ka->...ab", untwist_re, cos_small, precision=highest) - jnp.einsum(
        "...kb,ka->...ab", untwist_im, sin_small, precision=highest
    )
    result = result / length
    return result.reshape(result.shape[:-2] + (length,))


def ray_weights(shifts, near_weight, far_weight, row_count, forward_sense):
    out_rows = lax.broadcasted_iota(jnp.int32, (1, 1, row_count, 1), 2)
    in_rows = lax.broadcasted_iota(jnp.int32, (1, 1, 1, row_count + 2 * HALO), 3)
    shift_grid = shifts[:, :, None, None]
    if forward_sense:
        near_hit = out_rows + shift_grid + HALO
        far_hit = near_hit + 1
    else:
        near_hit = out_rows - shift_grid + HALO
        far_hit = near_hit - 1
    near_part = near_weight[:, :, None, None] * (in_rows == near_hit).astype(jnp.float32)
    far_part = far_weight[:, :, None, None] * (in_rows == far_hit).astype(jnp.float32)
    return near_part + far_part


def row_mask(residual, first_row, total_rows):
    global_row = first_row + lax.broadcasted_iota(jnp.int32, (1, residual.shape[1], 1), 1)
    inside = (global_row >= 0) & (global_row < total_rows)
    return jnp.where(inside, residual, 0.0)


def body(volume, measured, ray_offset, defocus):
    tilt_count, row_width, line_length = measured.shape
    layer_count = volume.shape[0]
    slab_count = lax.axis_size("gz")
    slab_index = lax.axis_index("gz")
    tile_index = lax.axis_index("xy")
    total_rows = row_width * lax.axis_size("xy")
    ray_norm = float(layer_count * slab_count) ** (-0.5)
    offsets = lax.dynamic_slice_in_dim(ray_offset, slab_index * layer_count, layer_count, 1)
    shifts = offsets // 8
    far_weight = (offsets % 8).astype(jnp.float32) / 8.0
    near_weight = 1.0 - far_weight
    padded = extended(volume, (("xy", 1),), HALO)
    first_row = tile_index * row_width
    forward = ray_weights(shifts.T, near_weight.T, far_weight.T, row_width, True)
    forward = jnp.transpose(forward, (1, 0, 2, 3))
    partial_value = jnp.einsum("tzxa,zay->txy", forward, padded, precision=highest)
    response = ctf_response(defocus, line_length)
    summed = lax.psum(partial_value, "gz")
    residual = row_mask(measured - ray_norm * summed, first_row, total_rows)
    slab_response = lax.dynamic_index_in_dim(response, slab_index, 1, keepdims=False)
    own_slab = ctf_filter(residual, slab_response[:, None])
    own_slab = extended(own_slab, (("xy", 1),), HALO)
    backward = ray_weights(shifts.T, near_weight.T, far_weight.T, row_width, False)
    update = jnp.einsum("ztxa,tay->zxy", backward, own_slab, precision=highest)
    return volume + update / tilt_count


def solution(mesh):
    placed = (P("gz", "xy", None), P(None, "xy", None), P(), P())
    return jax.shard_map(
        body, mesh=mesh, in_specs=placed, out_specs=P("gz", "xy", None), check_vma=False
    )
```

profile of v0, /device:TPU:185, one launch (start us, length us, event | category | flops | bytes accessed | tf_op | source)
XLA Modules:
  0.0 232.3 jit_solution(7526004834016617804)
XLA Ops:
  6.5 0.0 copy-start.1
  6.5 0.0 copy-start.2
  6.5 0.0 all-reduce.2.cloned.1.call-start
  6.5 1.4 fusion.164
  7.9 6.2 %collective-permute-start = (f32[4,16,2048]{2,1,0:T(8,128)S(1)}, f32[4,16,2048]{2,1,0:T(8,128)S(1)}, u32[]{:S(2)}, u32[]{:S(2)}) collective-permute-start(f32[4,16,2048]{2,1,0:T(8,128)S(1)} %get-tuple-element.9), channel_id=1, source_target_pairs={{0,16},{16,32},{32,48},{48,64},{64,80},{80,96},{96,112},{112,128},... | collective-permute-start | bytes 1572872 | tf_op jit(solution)/shard_map/ppermute | solution.py:26
  14.2 1.9 collective-permute-start.1
  16.1 0.0 copy-done.2
  16.1 0.1 fusion.161
  16.2 0.1 add_select_fusion.5
  16.3 0.1 fusion.91
  16.3 16.1 %collective-permute-done = f32[4,16,2048]{2,1,0:T(8,128)S(1)} collective-permute-done((f32[4,16,2048]{2,1,0:T(8,128)S(1)}, f32[4,16,2048]{2,1,0:T(8,128)S(1)}, u32[]{:S(2)}, u32[]{:S(2)}) %collective-permute-start) | collective-permute-done | bytes 524320 | tf_op jit(solution)/shard_map/ppermute | solution.py:26
  32.4 8.9 %collective-permute-done.1 = f32[4,16,2048]{2,1,0:T(8,128)} collective-permute-done((f32[4,16,2048]{2,1,0:T(8,128)S(1)}, f32[4,16,2048]{2,1,0:T(8,128)}, u32[]{:S(2)}, u32[]{:S(2)}) %collective-permute-start.1) | collective-permute-done | bytes 524320 | tf_op jit(solution)/shard_map/ppermute | solution.py:28
  41.3 0.0 copy-done.1
  41.3 3.4 %convolution_bitcast_fusion.1 = f32[4,32,2048]{2,1,0:T(8,128)} fusion(f32[4,16,2048]{2,1,0:T(8,128)} %collective-permute-done.1, f32[4,32,2048]{2,1,0:T(8,128)S(1)} %copy-done.1, f32[4,16,2048]{2,1,0:T(8,128)S(1)} %collective-permute-done, f32[4,4]{1,0:T(4,128)S(1)} %get-tuple-element.6, s32[4,4,32]{2,1,0:T(4,128)S(1)} %get-tuple-element.14, ...), kind=kOutput, calls=%fused_computation.3 | convolution fusion | flops 806518784 | bytes 3149952 | tf_op jit(solution)/shard_map/tzxa,zay->txy/dot_general | solution.py:127
  44.7 0.0 copy-start.3
  44.7 0.0 copy-start
  44.8 0.0 all-reduce.2.cloned.1.call-update
  44.8 0.7 copy-done.3
  45.4 0.1 copy.8
  45.5 0.1 fusion.98
  45.6 0.2 negate_bitcast_fusion
  45.8 128.7 %all-reduce.2.cloned.1.call-done = f32[4,32,2048]{2,1,0:T(8,128)} async-done(((f32[4,32,2048]{2,1,0:T(8,128)}), f32[4,32,2048]{2,1,0:T(8,128)}) %all-reduce.2.cloned.1.call-update) | async-done | bytes 1048592 | tf_op jit(solution)/shard_map/psum | solution.py:129
  174.5 0.0 copy-done
  174.5 1.4 subtract_select_fusion
  176.0 0.2 copy.15
  176.2 1.0 convolution_negate_fusion
  177.2 1.0 fusion.15
  178.3 1.2 fusion.21
  179.5 1.2 fusion.17
  180.7 1.2 fusion.13
  182.0 1.2 fusion.60
  183.2 1.2 fusion.12
  184.5 1.2 fusion.57
  185.7 1.4 convolution_subtract_fusion.1
  187.1 1.2 convolution_add_fusion
  188.3 1.1 fusion.26
  189.4 1.1 fusion.11
  190.5 0.2 reshape.102
  190.6 0.1 fusion.163
  190.7 4.5 %collective-permute-start.2 = (f32[4,16,2048]{2,1,0:T(8,128)S(1)}, f32[4,16,2048]{2,1,0:T(8,128)}, u32[]{:S(2)}, u32[]{:S(2)}) collective-permute-start(f32[4,16,2048]{2,1,0:T(8,128)S(1)} %get-tuple-element.7), channel_id=1, source_target_pairs={{0,16},{16,32},{32,48},{48,64},{64,80},{80,96},{96,112},{112,128},... | collective-permute-start | bytes 1572872 | tf_op jit(solution)/shard_map/ppermute | solution.py:26
  195.3 1.9 collective-permute-start.3
  197.2 0.1 copy.7
  197.3 0.1 fusion.169
  197.4 0.1 copy.5
  197.5 0.1 copy.6
  197.5 0.1 fusion.95
  197.6 14.4 %collective-permute-done.2 = f32[4,16,2048]{2,1,0:T(8,128)} collective-permute-done((f32[4,16,2048]{2,1,0:T(8,128)S(1)}, f32[4,16,2048]{2,1,0:T(8,128)}, u32[]{:S(2)}, u32[]{:S(2)}) %collective-permute-start.2) | collective-permute-done | bytes 524320 | tf_op jit(solution)/shard_map/ppermute | solution.py:26
  212.1 9.8 %collective-permute-done.3 = f32[4,16,2048]{2,1,0:T(8,128)} collective-permute-done((f32[4,16,2048]{2,1,0:T(8,128)S(1)}, f32[4,16,2048]{2,1,0:T(8,128)}, u32[]{:S(2)}, u32[]{:S(2)}) %collective-permute-start.3) | collective-permute-done | bytes 524320 | tf_op jit(solution)/shard_map/ppermute | solution.py:28
  221.9 3.6 %fusion.1 = f32[4,32,2048]{2,1,0:T(8,128)} fusion(f32[4,32,2048]{2,1,0:T(8,128)S(1)} %copy-done.1, f32[4,16,2048]{2,1,0:T(8,128)} %collective-permute-done.3, f32[4,32,2048]{2,1,0:T(8,128)S(1)} %reshape.102, f32[4,16,2048]{2,1,0:T(8,128)} %collective-permute-done.2, f32[4,4]{1,0:T(4,128)S(1)} %copy.7, s32[4,4,32]{2,1,0:T(4,128)S(1)} %get-tuple-element.12, ...), kind=kOutput, calls=%fused_computation.2 | convolution fusion | flops 807043072 | bytes 4198528 | tf_op jit(solution)/shard_map/ztxa,tay->zxy/dot_general | solution.py:135
  (6 shorter events, 0.0 us)
Async XLA Ops:
  6.5 34.8 %copy-start.1 = (f32[4,32,2048]{2,1,0:T(8,128)S(1)}, f32[4,32,2048]{2,1,0:T(8,128)}, u32[]{:S(2)}) copy-start(f32[4,32,2048]{2,1,0:T(8,128)} %param.4) | copy-start | bytes 3145732
  6.5 9.6 %copy-start.2 = (s32[4,64]{1,0:T(4,128)S(1)}, s32[4,64]{1,0:T(4,128)}, u32[]{:S(2)}) copy-start(s32[4,64]{1,0:T(4,128)} %param.6) | copy-start | bytes 3076
  6.5 168.0 %all-reduce.2.cloned.1.call-start = ((), (), s32[]{:S(2)}) async-start(), calls=%async_computation | async-start | bytes 2097152 | tf_op jit(solution)/shard_map/psum | solution.py:129
  7.9 24.5 %collective-permute-start = (f32[4,16,2048]{2,1,0:T(8,128)S(1)}, f32[4,16,2048]{2,1,0:T(8,128)S(1)}, u32[]{:S(2)}, u32[]{:S(2)}) collective-permute-start(f32[4,16,2048]{2,1,0:T(8,128)S(1)} %get-tuple-element.9), channel_id=1, source_target_pairs={{0,16},{16,32},{32,48},{48,64},{64,80},{80,96},{96,112},{112,128},... | collective-permute-start | bytes 1572872 | tf_op jit(solution)/shard_map/ppermute | solution.py:26
  14.2 27.1 %collective-permute-start.1 = (f32[4,16,2048]{2,1,0:T(8,128)S(1)}, f32[4,16,2048]{2,1,0:T(8,128)}, u32[]{:S(2)}, u32[]{:S(2)}) collective-permute-start(f32[4,16,2048]{2,1,0:T(8,128)S(1)} %get-tuple-element.10), channel_id=1, source_target_pairs={{16,0},{32,16},{48,32},{64,48},{80,64},{96,80},{112,96},{128,112},... | collective-permute-start | bytes 1572872 | tf_op jit(solution)/shard_map/ppermute | solution.py:28
  44.7 0.7 copy-start.3
  44.7 129.8 %copy-start = (f32[4,32,2048]{2,1,0:T(8,128)S(1)}, f32[4,32,2048]{2,1,0:T(8,128)}, u32[]{:S(2)}) copy-start(f32[4,32,2048]{2,1,0:T(8,128)} %param.5) | copy-start | bytes 3145732
  190.7 21.3 %collective-permute-start.2 = (f32[4,16,2048]{2,1,0:T(8,128)S(1)}, f32[4,16,2048]{2,1,0:T(8,128)}, u32[]{:S(2)}, u32[]{:S(2)}) collective-permute-start(f32[4,16,2048]{2,1,0:T(8,128)S(1)} %get-tuple-element.7), channel_id=1, source_target_pairs={{0,16},{16,32},{32,48},{48,64},{64,80},{80,96},{96,112},{112,128},... | collective-permute-start | bytes 1572872 | tf_op jit(solution)/shard_map/ppermute | solution.py:26
  195.3 26.6 %collective-permute-start.3 = (f32[4,16,2048]{2,1,0:T(8,128)S(1)}, f32[4,16,2048]{2,1,0:T(8,128)}, u32[]{:S(2)}, u32[]{:S(2)}) collective-permute-start(f32[4,16,2048]{2,1,0:T(8,128)S(1)} %get-tuple-element.8), channel_id=1, source_target_pairs={{16,0},{32,16},{48,32},{64,48},{80,64},{96,80},{112,96},{128,112},... | collective-permute-start | bytes 1572872 | tf_op jit(solution)/shard_map/ppermute | solution.py:28
Sparse Core Ops, SparseCore 0:
  44.9 129.5 all-reduce.1
where the time goes:
time: 235 us; the launch traced here: 232 us
  waiting for transfers between devices  178 us (76%)
  matrix products  21.3 us (9%)
  starting transfers between devices  14.6 us (6%)
  between operations  13.6 us (6%)
  local copies, waits for them, and re-layouts  2.85 us (1%)
    psum x1, waiting for transfers between devices, body(): summed = lax.psum(partial_value, 'gz')  129 us
    ppermute x2, waiting for transfers between devices, extended(): lax.ppermute(tail, axis, [(i, (i + 1) % count) for i in range(ends)])  30.5 us
    ppermute x2, waiting for transfers between devices, extended(): lax.ppermute(head, axis, [((i + 1) % count, i) for i in range(ends)])  18.7 us
    ppermute x2, starting transfers between devices, extended(): lax.ppermute(tail, axis, [(i, (i + 1) % count) for i in range(ends)])  10.7 us
  transfers between devices with their start and end apart: 5, of which 5 were waited for; matrix products, arithmetic and copies ran while one was open for 0% of the time, Pallas kernels for 0%

commit v1 on v0

v1 whole, which is shorter than its diff:
```python
import functools
import math

import jax
import jax.numpy as jnp
import ml_dtypes
import numpy as np
from jax import lax
from jax.experimental import pallas as pl
from jax.experimental.pallas import tpu as pltpu
from jax.sharding import PartitionSpec as P

HALO = 16
LINE = 2048
PART = 256
ROWS = 32
LAYERS = 4
TILTS = 4

pixel_size = 4.0
wavelength = 0.0197
contrast = 0.07
amplitude_root = math.sqrt(1.0 - 0.07 * 0.07)
f32 = jnp.float32
bf16 = jnp.bfloat16
MESH = pl.DeviceIdType.MESH

GROUPS = ((0, 256, 0), (256, 256, 4), (512, 512, 1), (1024, 512, 2), (1536, 512, 3))


def halves(table):
    high = table.astype(ml_dtypes.bfloat16)
    low = (table - high.astype(np.float64)).astype(ml_dtypes.bfloat16)
    return np.stack([high, low])


def dft_tables():
    b = np.arange(PART, dtype=np.int64)[:, None]
    tables, freq, scale = {}, [], []
    for _, width, residue in GROUPS:
        if residue == 0:
            re, im = np.arange(0, 129), np.arange(1, 128)
        elif residue == 4:
            re = im = np.arange(0, 128)
        else:
            re = im = np.arange(0, 256)
        f_re, f_im = residue + 8 * re, residue + 8 * im
        turn_re = 2 * np.pi / LINE * (b * f_re % LINE)
        turn_im = 2 * np.pi / LINE * (b * f_im % LINE)
        real_in = np.concatenate([np.cos(turn_re), -np.sin(turn_im)], 1)
        if width == 512:
            imag_in = np.concatenate([np.sin(turn_re), np.cos(turn_im)], 1)
            real_in = np.concatenate([real_in, imag_in], 0)
        tables[residue] = real_in
        f = np.concatenate([f_re, f_im])
        folded = np.where(2 * f < LINE, f, f - LINE)
        freq.append(folded / (LINE * pixel_size))
        scale.append(np.where((f == 0) | (f == LINE // 2), 1.0, 2.0) / (LINE * TILTS))
    big = np.stack([tables[1], tables[2], tables[3]])
    small = np.stack([tables[0], tables[4]])
    line = np.stack([np.concatenate(freq), np.concatenate(scale)]).astype(np.float32)
    return (
        halves(big),
        halves(small),
        halves(big.transpose(0, 2, 1)),
        halves(small.transpose(0, 2, 1)),
        line,
    )


def split(x):
    high = x.astype(bf16)
    low = (x - high.astype(f32)).astype(bf16)
    return high, low


def dot(a, b):
    return jnp.dot(a, b, preferred_element_type=f32)


def kernel(
    tiles,
    ray,
    defocus,
    vol,
    meas,
    line,
    fwd_big_hbm,
    fwd_small_hbm,
    inv_big_hbm,
    inv_small_hbm,
    out,
    fwd_big,
    fwd_small,
    inv_big,
    inv_small,
    meas_own,
    vcat,
    other_g,
    other_o,
    mine_g,
    mine_o,
    core_g,
    core_o,
    relay_g,
    fin_g,
    zin_g,
    zin_o,
    relay_o,
    fin_o,
    halo_in,
    gathered,
    spectral,
    local_sem,
    ss,
    rs,
):
    gz = lax.axis_index("gz")
    xy = lax.axis_index("xy")
    X = gz // 4
    zl = (gz // 2) % 2
    c = gz % 2
    to_core = {"gz": gz + 1 - 2 * c}
    to_z = {"gz": gz + 2 - 4 * zl}
    to_right = {"gz": (gz + 4) % 16}
    to_left = {"gz": (gz + 12) % 16}
    step = 1 - 2 * zl
    to_ahead = {"xy": (xy + step + tiles) % tiles}
    to_behind = {"xy": (xy - step + tiles) % tiles}
    partners = (to_core, to_z, to_right, to_left, to_ahead, to_behind)
    barrier = pltpu.get_barrier_semaphore()
    for partner in partners:
        pl.semaphore_signal(barrier, inc=1, device_id=partner, device_id_type=MESH)

    k_own = zl * 2 + c
    locals_ = [
        pltpu.make_async_copy(meas.at[X, pl.ds(pl.multiple_of(8 * k_own, 8), 8)], meas_own, local_sem.at[0]),
        pltpu.make_async_copy(fwd_big_hbm, fwd_big, local_sem.at[1]),
        pltpu.make_async_copy(fwd_small_hbm, fwd_small, local_sem.at[2]),
        pltpu.make_async_copy(inv_big_hbm, inv_big, local_sem.at[3]),
        pltpu.make_async_copy(inv_small_hbm, inv_small, local_sem.at[4]),
    ]
    for copy in locals_:
        copy.start()

    count = [0]
    sent = []

    def send(src, dst, where):
        i = count[0]
        count[0] += 1
        copy = pltpu.make_async_remote_copy(
            src_ref=src, dst_ref=dst, send_sem=ss.at[i], recv_sem=rs.at[i],
            device_id=where, device_id_type=MESH,
        )
        copy.start()
        sent.append(copy)
        return copy

    shift, far = {}, {}
    for dt in range(4):
        t = (X + dt) % 4
        for z in range(LAYERS):
            offset = ray[t, gz * LAYERS + z]
            shift[dt, z] = offset >> 3
            far[dt, z] = (offset & 7).astype(f32) * 0.125

    col = lax.broadcasted_iota(jnp.int32, (8, 128), 1)
    sub = lax.broadcasted_iota(jnp.int32, (8, 128), 0)
    layer = col // ROWS
    target, near_row, far_row = {}, {}, {}
    for dt in range(4):
        s = jnp.zeros((8, 128), jnp.int32)
        w = jnp.zeros((8, 128), f32)
        for z in range(LAYERS):
            s = jnp.where(layer == z, shift[dt, z], s)
            w = jnp.where(layer == z, far[dt, z], w)
        target[dt] = col % ROWS - s
        near_row[dt], far_row[dt] = 1.0 - w, w

    def first_ext(zone, core, ghost):
        base = 8 * (zone * 2 + core)
        if ghost:
            base = base + 32 - 64 * zone
        return base

    def weights(core, ghost, dt, dzl):
        zone = zl ^ dzl
        e = sub + first_ext(zone, core, ghost)
        return jnp.where(e == target[dt], near_row[dt], 0.0) + jnp.where(
            e == target[dt] - 1, far_row[dt], 0.0
        )

    def lhs(core):
        blocks = [weights(core, True, dt, dzl) for dt in range(4) for dzl in range(2)]
        blocks += [weights(core, False, dt, dzl) for dzl in range(2) for dt in range(4)]
        w = jnp.concatenate(blocks, 0).astype(bf16)
        return jnp.concatenate([w, w], 1)

    volume = vol[...].reshape(LAYERS * ROWS, LINE)
    vh, vl = split(volume)
    vcat[0:128, :] = vh
    vcat[128:256, :] = vl

    def project(core, to_g, to_o):
        w = lhs(core)
        for j in range(4):
            at = pl.ds(512 * j, 512)
            p = dot(w, vcat[:, at])
            to_g[:, :, :, at] = p[0:64].reshape(4, 2, 8, 512)
            to_o[:, :, :, at] = p[64:128].reshape(2, 4, 8, 512)

    project(1 - c, other_g, other_o)
    pl.semaphore_wait(barrier, len(partners))
    cg, co = {}, {}
    cg[2] = send(other_g.at[2], core_g.at[2], to_core)
    co[1] = send(other_o.at[1], core_o.at[1], to_core)
    cg[1] = send(other_g.at[1], core_g.at[1], to_core)
    cg[3] = send(other_g.at[3], core_g.at[3], to_core)
    co[0] = send(other_o.at[0], core_o.at[0], to_core)
    cg[0] = send(other_g.at[0], core_g.at[0], to_core)
    project(c, mine_g, mine_o)

    def add(dst, src):
        dst[...] = dst[...] + src[...]

    half = (pl.ds(0, 1024), pl.ds(1024, 1024))
    cg[2].wait_recv()
    add(mine_g.at[2], core_g.at[2])
    g_relay_right = send(mine_g.at[2, 0], relay_g.at[0], to_right)
    g_relay_left = send(mine_g.at[2, 1], relay_g.at[1], to_left)
    co[1].wait_recv()
    add(mine_o.at[1], core_o.at[1])
    oz = {}
    for dt in (2, 1, 3, 0):
        oz[dt] = send(mine_o.at[1, dt], zin_o.at[dt], to_z)
    cg[1].wait_recv()
    add(mine_g.at[1], core_g.at[1])
    g_plain_right = send(mine_g.at[1, 1], fin_g.at[0, 1], to_right)
    cg[3].wait_recv()
    add(mine_g.at[3], core_g.at[3])
    g_plain_left = send(mine_g.at[3, 0], fin_g.at[1, 0], to_left)
    co[0].wait_recv()
    add(mine_o.at[0], core_o.at[0])
    cg[0].wait_recv()
    add(mine_g.at[0], core_g.at[0])

    g_relay_right.wait_recv()
    add(mine_g.at[1, 0], relay_g.at[0])
    g_fin_right = send(mine_g.at[1, 0], fin_g.at[0, 0], to_right)
    g_relay_left.wait_recv()
    add(mine_g.at[3, 1], relay_g.at[1])
    g_fin_left = send(mine_g.at[3, 1], fin_g.at[1, 1], to_left)

    oz[2].wait_recv()
    add(mine_o.at[0, 2], zin_o.at[2])
    o_relay_right = send(mine_o.at[0, 2, :, half[0]], relay_o.at[0], to_right)
    o_relay_left = send(mine_o.at[0, 2, :, half[1]], relay_o.at[1], to_left)
    oz[1].wait_recv()
    add(mine_o.at[0, 1], zin_o.at[1])
    o_plain_right = send(mine_o.at[0, 1, :, half[1]], fin_o.at[0, :, half[1]], to_right)
    oz[3].wait_recv()
    add(mine_o.at[0, 3], zin_o.at[3])
    o_plain_left = send(mine_o.at[0, 3, :, half[0]], fin_o.at[1, :, half[0]], to_left)

    g_plain_right.wait_recv()
    g_plain_left.wait_recv()
    g_fin_right.wait_recv()
    g_fin_left.wait_recv()
    mine_g[0] = mine_g[0] + fin_g[0] + fin_g[1]
    gz_copy = send(mine_g.at[0, 1], zin_g, to_z)

    o_relay_right.wait_recv()
    add(mine_o.at[0, 1, :, half[0]], relay_o.at[0])
    o_fin_right = send(mine_o.at[0, 1, :, half[0]], fin_o.at[0, :, half[0]], to_right)
    o_relay_left.wait_recv()
    add(mine_o.at[0, 3, :, half[1]], relay_o.at[1])
    o_fin_left = send(mine_o.at[0, 3, :, half[1]], fin_o.at[1, :, half[1]], to_left)

    gz_copy.wait_recv()
    add(mine_g.at[0, 0], zin_g)
    halo = send(mine_g.at[0, 0], halo_in, to_ahead)

    oz[0].wait_recv()
    o_plain_right.wait_recv()
    o_plain_left.wait_recv()
    o_fin_right.wait_recv()
    o_fin_left.wait_recv()
    total = mine_o[0, 0] + zin_o[0] + fin_o[0] + fin_o[1]
    for copy in locals_:
        copy.wait()
    halo.wait_recv()
    behind = xy - step
    inside = (behind >= 0) & (behind < tiles)
    total = total + jnp.where(inside, halo_in[...], 0.0)
    ray_norm = float(TILTS * 16) ** (-0.5)
    residual = meas_own[...] - ray_norm * total

    x = [residual[:, PART * a : PART * (a + 1)] for a in range(8)]
    root = math.sqrt(0.5)
    s04, d04 = x[0] + x[4], x[0] - x[4]
    s26, d26 = x[2] + x[6], x[2] - x[6]
    s15, d15 = x[1] + x[5], x[1] - x[5]
    s37, d37 = x[3] + x[7], x[3] - x[7]
    even, odd = s04 + s26, s15 + s37
    m = root * (d15 - d37)
    n = root * (d15 + d37)
    inputs = {
        0: even + odd,
        4: even - odd,
        1: jnp.concatenate([d04 + m, -(d26 + n)], 1),
        2: jnp.concatenate([s04 - s26, s37 - s15], 1),
        3: jnp.concatenate([d04 - m, d26 - n], 1),
    }
    for first, width, residue in GROUPS:
        high, low = split(inputs[residue])
        if width == 512:
            th, tl = fwd_big[0, residue - 1], fwd_big[1, residue - 1]
        else:
            th, tl = fwd_small[0, residue // 4], fwd_small[1, residue // 4]
        both = dot(jnp.concatenate([high, low], 0), th)
        gathered[0, 0, 0, 0, :, first : first + width] = both[0:8] + both[8:16] + dot(high, tl)

    own = gathered.at[0, 0, 0, 0]
    a_halo = send(own, gathered.at[0, 0, 0, 1], to_behind)
    ar = send(own, gathered.at[0, 3, 0, 0], to_right)
    al = send(own, gathered.at[0, 1, 0, 0], to_left)
    az = {0: [send(own, gathered.at[0, 0, 1, 0], to_z)]}
    cores = []

    def to_other(dt, dzl, ghost):
        cores.append(send(gathered.at[0, dt, dzl, ghost], gathered.at[1, dt, dzl, ghost], to_core))

    to_other(0, 0, 0)
    ar.wait_recv()
    arr = send(gathered.at[0, 3, 0, 0, :, half[0]], gathered.at[0, 2, 0, 0, :, half[0]], to_right)
    az[3] = [send(gathered.at[0, 3, 0, 0], gathered.at[0, 3, 1, 0], to_z)]
    al.wait_recv()
    arl = send(gathered.at[0, 1, 0, 0, :, half[1]], gathered.at[0, 2, 0, 0, :, half[1]], to_left)
    az[1] = [send(gathered.at[0, 1, 0, 0], gathered.at[0, 1, 1, 0], to_z)]
    a_halo.wait_recv()
    gzc = send(gathered.at[0, 0, 0, 1], gathered.at[0, 0, 1, 1], to_z)
    gr0 = send(gathered.at[0, 0, 0, 1], gathered.at[0, 3, 0, 1], to_right)
    gl0 = send(gathered.at[0, 0, 0, 1], gathered.at[0, 1, 0, 1], to_left)
    to_other(3, 0, 0)
    to_other(1, 0, 0)
    to_other(0, 0, 1)
    arr.wait_recv()
    arl.wait_recv()
    az[2] = [send(gathered.at[0, 2, 0, 0], gathered.at[0, 2, 1, 0], to_z)]
    to_other(2, 0, 0)
    gzc.wait_recv()
    gr1 = send(gathered.at[0, 0, 1, 1], gathered.at[0, 3, 1, 1], to_right)
    gl1 = send(gathered.at[0, 0, 1, 1], gathered.at[0, 1, 1, 1], to_left)
    to_other(0, 1, 1)
    az[0][0].wait_recv()
    to_other(0, 1, 0)
    gr0.wait_recv()
    grr = send(gathered.at[0, 3, 0, 1], gathered.at[0, 2, 0, 1], to_right)
    to_other(3, 0, 1)
    gl0.wait_recv()
    to_other(1, 0, 1)
    gl1.wait_recv()
    grl = send(gathered.at[0, 1, 1, 1], gathered.at[0, 2, 1, 1], to_left)
    to_other(1, 1, 1)
    gr1.wait_recv()
    to_other(3, 1, 1)
    az[3][0].wait_recv()
    to_other(3, 1, 0)
    az[1][0].wait_recv()
    to_other(1, 1, 0)

    frequency = line[0:1, :]
    ctf = []
    for dt in range(4):
        number = defocus[(X + dt) % 4, gz].astype(f32)
        phase = math.pi * wavelength * number * frequency * frequency
        ctf.append(
            -(amplitude_root * jnp.sin(phase) + contrast * jnp.cos(phase)) * line[1:2, :]
        )

    gcol = lax.broadcasted_iota(jnp.int32, (ROWS, 256), 1)
    grow = lax.broadcasted_iota(jnp.int32, (ROWS, 256), 0)
    zone = zl ^ ((gcol >> 4) & 1)
    place = 8 * (zone * 2 + (c ^ (gcol >> 7))) + (gcol & 7)
    place = place + ((gcol >> 3) & 1) * (32 - 64 * zone)
    tilt = (gcol >> 5) & 3
    there = place + xy * ROWS
    legal = (there >= 0) & (there < tiles * ROWS)
    back = []
    for z in range(LAYERS):
        s = jnp.zeros((ROWS, 256), jnp.int32)
        w = jnp.zeros((ROWS, 256), f32)
        for dt in range(4):
            s = jnp.where(tilt == dt, shift[dt, z], s)
            w = jnp.where(tilt == dt, far[dt, z], w)
        delta = place + s - grow
        both = jnp.where(delta == 0, 1.0 - w, 0.0) + jnp.where(delta == -1, w, 0.0)
        back.append(jnp.where(legal, both, 0.0))
    back = jnp.concatenate(back, 0).astype(bf16)

    az[2][0].wait_recv()
    to_other(2, 1, 0)
    grr.wait_recv()
    to_other(2, 0, 1)
    grl.wait_recv()
    to_other(2, 1, 1)
    for copy in cores:
        copy.wait_recv()

    for first, width, residue in GROUPS:
        at = pl.ds(first, width)
        highs, lows = [], []
        for dc in range(2):
            for dt in range(4):
                block = gathered[dc, dt, :, :, :, at].reshape(32, width)
                high, low = split(block * ctf[dt][:, first : first + width])
                highs.append(high)
                lows.append(low)
        u = dot(back, jnp.concatenate(highs, 0)) + dot(back, jnp.concatenate(lows, 0))
        high, low = split(u)
        if width == 512:
            th, tl = inv_big[0, residue - 1], inv_big[1, residue - 1]
        else:
            th, tl = inv_small[0, residue // 4], inv_small[1, residue // 4]
        spectral[:, at] = dot(high, th) + dot(low, th) + dot(high, tl)

    def part(first):
        return spectral[:, first : first + PART]

    g0, g4 = part(0), part(256)
    r1, i1, r2, i2, r3, i3 = (part(512 + PART * i) for i in range(6))
    p, q = g0 + g4, g0 - g4
    pr, ps = p + r2, p - r2
    qm, qp = q - i2, q + i2
    r13, i31 = r1 + r3, i3 - i1
    rd, im = r1 - r3, i1 + i3
    v, w = root * (rd - im), root * (rd + im)
    ys = (pr + r13, qm + v, ps + i31, qp - w, pr - r13, qm - v, ps - i31, qp + w)
    for a in range(8):
        at = pl.ds(PART * a, PART)
        out[:, :, at] = vol[:, :, at] + ys[a].reshape(LAYERS, ROWS, PART)

    for copy in sent:
        copy.wait_send()


def body(tiles, tables, volume, measured, ray_offset, defocus):
    fwd_big, fwd_small, inv_big, inv_small, line = tables
    vmem = pl.BlockSpec(memory_space=pltpu.VMEM)
    smem = pl.BlockSpec(memory_space=pltpu.SMEM)
    anywhere = pl.BlockSpec(memory_space=pl.ANY)

    def f(*shape):
        return pltpu.VMEM(shape, f32)

    return pl.pallas_call(
        functools.partial(kernel, tiles),
        out_shape=jax.ShapeDtypeStruct(volume.shape, f32),
        in_specs=[smem, smem, vmem, anywhere, vmem, anywhere, anywhere, anywhere, anywhere],
        out_specs=vmem,
        scratch_shapes=[
            pltpu.VMEM(fwd_big.shape, bf16),
            pltpu.VMEM(fwd_small.shape, bf16),
            pltpu.VMEM(inv_big.shape, bf16),
            pltpu.VMEM(inv_small.shape, bf16),
            f(8, LINE),
            pltpu.VMEM((256, LINE), bf16),
            f(4, 2, 8, LINE),
            f(2, 4, 8, LINE),
            f(4, 2, 8, LINE),
            f(2, 4, 8, LINE),
            f(4, 2, 8, LINE),
            f(2, 4, 8, LINE),
            f(2, 8, LINE),
            f(2, 2, 8, LINE),
            f(8, LINE),
            f(4, 8, LINE),
            f(2, 8, LINE // 2),
            f(2, 8, LINE),
            f(8, LINE),
            f(2, 4, 2, 2, 8, LINE),
            f(128, LINE),
            pltpu.SemaphoreType.DMA((5,)),
            pltpu.SemaphoreType.DMA((64,)),
            pltpu.SemaphoreType.DMA((64,)),
        ],
        compiler_params=pltpu.CompilerParams(
            collective_id=0, has_side_effects=True, vmem_limit_bytes=48 * 1024 * 1024
        ),
        name="step",
    )(ray_offset, defocus, volume, measured, line, fwd_big, fwd_small, inv_big, inv_small)


def solution(mesh):
    placed = (P("gz", "xy", None), P(None, "xy", None), P(), P())
    tables = tuple(dft_tables())
    return jax.shard_map(
        functools.partial(body, mesh.shape["xy"], tables),
        mesh=mesh,
        in_specs=placed,
        out_specs=P("gz", "xy", None),
        check_vma=False,
    )
```

time: 235 us -> 61.5 us (0.26)
  the two profiles are of different devices: /device:TPU:185 before, /device:TPU:1 now
where the time goes in v1:
time: 61.5 us; the launch traced here: 61.1 us
  Pallas kernels  53.5 us (87%)
  local copies, waits for them, and re-layouts  7.58 us (12%)
    pallas_call x1, Pallas kernels, body(): pl.pallas_call(functools.partial(kernel, tiles), out_shape=jax.ShapeDtype...  53.5 us
    unnamed x15, local copies, waits for them, and re-layouts  7.58 us

profile of v1, /device:TPU:1, one launch (start us, length us, event | category | flops | bytes accessed | tf_op | source)
XLA Modules:
  0.0 61.1 jit_solution(13990663921659873116)
XLA Ops:
  0.0 0.0 copy-start
  0.0 1.2 %copy-done = f32[4,32,2048]{2,1,0:T(8,128)S(1)} copy-done((f32[4,32,2048]{2,1,0:T(8,128)S(1)}, f32[4,32,2048]{2,1,0:T(8,128)}, u32[]{:S(2)}) %copy-start) | copy-done | bytes 1048600
  1.2 0.0 copy-start.1
  1.2 1.2 %copy-done.1 = f32[4,32,2048]{2,1,0:T(8,128)S(1)} copy-done((f32[4,32,2048]{2,1,0:T(8,128)S(1)}, f32[4,32,2048]{2,1,0:T(8,128)}, u32[]{:S(2)}) %copy-start.1) | copy-done | bytes 1048600
  2.5 0.0 copy-start.2
  2.5 1.0 %copy-done.2 = bf16[2,2,256,256]{3,2,1,0:T(8,128)(2,1)S(1)} copy-done((bf16[2,2,256,256]{3,2,1,0:T(8,128)(2,1)S(1)}, bf16[2,2,256,256]{3,2,1,0:T(8,128)(2,1)}, u32[]{:S(2)}) %copy-start.2) | copy-done | bytes 524312
  3.5 0.0 copy-start.3
  3.5 1.0 %copy-done.3 = bf16[2,2,256,256]{3,2,1,0:T(8,128)(2,1)S(1)} copy-done((bf16[2,2,256,256]{3,2,1,0:T(8,128)(2,1)S(1)}, bf16[2,2,256,256]{3,2,1,0:T(8,128)(2,1)}, u32[]{:S(2)}) %copy-start.3) | copy-done | bytes 524312
  4.5 0.0 copy-start.4
  4.5 0.7 %copy-done.4 = f32[2,2048]{1,0:T(2,128)S(1)} copy-done((f32[2,2048]{1,0:T(2,128)S(1)}, f32[2,2048]{1,0:T(2,128)}, u32[]{:S(2)}) %copy-start.4) | copy-done | bytes 16408
  5.3 0.0 copy-start.5
  5.3 0.7 %copy-done.5 = s32[4,64]{1,0:T(4,128)S(1)} copy-done((s32[4,64]{1,0:T(4,128)S(1)}, s32[4,64]{1,0:T(4,128)}, u32[]{:S(2)}) %copy-start.5) | copy-done | bytes 1048
  5.9 0.0 copy-start.6
  5.9 0.7 %copy-done.6 = s32[4,16]{1,0:T(4,128)S(1)} copy-done((s32[4,16]{1,0:T(4,128)S(1)}, s32[4,16]{1,0:T(4,128)}, u32[]{:S(2)}) %copy-start.6) | copy-done | bytes 280
  6.6 53.5 %step.1 = f32[4,32,2048]{2,1,0:T(8,128)S(1)} custom-call(s32[4,64]{1,0:T(4,128)S(1)} %copy-done.5, s32[4,16]{1,0:T(4,128)S(1)} %copy-done.6, f32[4,32,2048]{2,1,0:T(8,128)S(1)} %copy-done, f32[4,32,2048]{2,1,0:T(8,128)S(1)} %copy-done.1, f32[2,2048]{1,0:T(2,128)S(1)} %copy-done.4, bf16[2,3,512,512]{3,2,1,0:T(8,128)(2,1)} %constant.11.clone.fwd_big_hbm, ...), custom_call_target="tpu_custom_call" | custom-call | tf_op jit(solution)/shard_map/step/pallas_call | solution.py:457
  60.1 1.0 %copy.11 = f32[4,32,2048]{2,1,0:T(8,128)} copy(f32[4,32,2048]{2,1,0:T(8,128)S(1)} %step.1) | data formatting | bytes 2097152
Async XLA Ops:
  0.0 1.2 %copy-start = (f32[4,32,2048]{2,1,0:T(8,128)S(1)}, f32[4,32,2048]{2,1,0:T(8,128)}, u32[]{:S(2)}) copy-start(f32[4,32,2048]{2,1,0:T(8,128)} %vol.1) | copy-start | bytes 3145732
  1.2 1.2 %copy-start.1 = (f32[4,32,2048]{2,1,0:T(8,128)S(1)}, f32[4,32,2048]{2,1,0:T(8,128)}, u32[]{:S(2)}) copy-start(f32[4,32,2048]{2,1,0:T(8,128)} %meas.1) | copy-start | bytes 3145732
  2.5 1.0 %copy-start.2 = (bf16[2,2,256,256]{3,2,1,0:T(8,128)(2,1)S(1)}, bf16[2,2,256,256]{3,2,1,0:T(8,128)(2,1)}, u32[]{:S(2)}) copy-start(bf16[2,2,256,256]{3,2,1,0:T(8,128)(2,1)} %constant.14.clone.inv_small_hbm) | copy-start | bytes 1572868
  3.5 1.0 %copy-start.3 = (bf16[2,2,256,256]{3,2,1,0:T(8,128)(2,1)S(1)}, bf16[2,2,256,256]{3,2,1,0:T(8,128)(2,1)}, u32[]{:S(2)}) copy-start(bf16[2,2,256,256]{3,2,1,0:T(8,128)(2,1)} %constant.12.clone.fwd_small_hbm) | copy-start | bytes 1572868
  4.5 0.7 %copy-start.4 = (f32[2,2048]{1,0:T(2,128)S(1)}, f32[2,2048]{1,0:T(2,128)}, u32[]{:S(2)}) copy-start(f32[2,2048]{1,0:T(2,128)} %constant.10.clone.line) | copy-start | bytes 49156
  5.3 0.7 %copy-start.5 = (s32[4,64]{1,0:T(4,128)S(1)}, s32[4,64]{1,0:T(4,128)}, u32[]{:S(2)}) copy-start(s32[4,64]{1,0:T(4,128)} %ray.1) | copy-start | bytes 3076
  5.9 0.7 %copy-start.6 = (s32[4,16]{1,0:T(4,128)S(1)}, s32[4,16]{1,0:T(4,128)}, u32[]{:S(2)}) copy-start(s32[4,16]{1,0:T(4,128)} %defocus.1) | copy-start | bytes 772

commit v2 on v1

v2 whole, which is shorter than its diff:
```python
import functools
import math

import jax
import jax.numpy as jnp
import ml_dtypes
import numpy as np
from jax import lax
from jax.experimental import pallas as pl
from jax.experimental.pallas import tpu as pltpu
from jax.sharding import PartitionSpec as P

HALO = 16
LINE = 2048
PART = 256
ROWS = 32
LAYERS = 4
TILTS = 4

pixel_size = 4.0
wavelength = 0.0197
contrast = 0.07
amplitude_root = math.sqrt(1.0 - 0.07 * 0.07)
f32 = jnp.float32
bf16 = jnp.bfloat16
MESH = pl.DeviceIdType.MESH

GROUPS = ((0, 256, 0), (256, 256, 4), (512, 512, 1), (1024, 512, 2), (1536, 512, 3))


def halves(table):
    high = table.astype(ml_dtypes.bfloat16)
    low = (table - high.astype(np.float64)).astype(ml_dtypes.bfloat16)
    return np.stack([high, low])


def dft_tables():
    b = np.arange(PART, dtype=np.int64)[:, None]
    tables, freq, scale = {}, [], []
    for _, width, residue in GROUPS:
        if residue == 0:
            re, im = np.arange(0, 129), np.arange(1, 128)
        elif residue == 4:
            re = im = np.arange(0, 128)
        else:
            re = im = np.arange(0, 256)
        f_re, f_im = residue + 8 * re, residue + 8 * im
        turn_re = 2 * np.pi / LINE * (b * f_re % LINE)
        turn_im = 2 * np.pi / LINE * (b * f_im % LINE)
        real_in = np.concatenate([np.cos(turn_re), -np.sin(turn_im)], 1)
        if width == 512:
            imag_in = np.concatenate([np.sin(turn_re), np.cos(turn_im)], 1)
            real_in = np.concatenate([real_in, imag_in], 0)
        tables[residue] = real_in
        f = np.concatenate([f_re, f_im])
        folded = np.where(2 * f < LINE, f, f - LINE)
        freq.append(folded / (LINE * pixel_size))
        scale.append(np.where((f == 0) | (f == LINE // 2), 1.0, 2.0) / (LINE * TILTS))
    big = np.stack([tables[1], tables[2], tables[3]])
    small = np.stack([tables[0], tables[4]])
    line = np.stack([np.concatenate(freq), np.concatenate(scale)]).astype(np.float32)
    return (
        halves(big),
        halves(small),
        halves(big.transpose(0, 2, 1)),
        halves(small.transpose(0, 2, 1)),
        line,
    )


def split(x):
    high = x.astype(bf16)
    low = (x - high.astype(f32)).astype(bf16)
    return high, low


def dot(a, b):
    return jnp.dot(a, b, preferred_element_type=f32)


def kernel(
    tiles,
    ray_hbm,
    defocus_hbm,
    vol_hbm,
    meas,
    line_hbm,
    fwd_big_hbm,
    fwd_small_hbm,
    inv_big_hbm,
    inv_small_hbm,
    out,
    ray,
    defocus,
    vol,
    line,
    response,
    back_rows,
    fwd_big,
    fwd_small,
    inv_big,
    inv_small,
    meas_rows,
    vcat,
    other_g,
    other_o,
    mine_g,
    mine_o,
    core_g,
    core_o,
    fin_g,
    zin_g,
    zin_o,
    fin_o,
    halo_g,
    halo_o,
    gathered,
    spectral,
    local_sem,
    ss,
    rs,
):
    gz = lax.axis_index("gz")
    xy = lax.axis_index("xy")
    X = gz // 4
    zl = (gz // 2) % 2
    c = gz % 2
    to_core = {"gz": gz + 1 - 2 * c}
    to_z = {"gz": gz + 2 - 4 * zl}
    to_right = {"gz": (gz + 4) % 16}
    to_left = {"gz": (gz + 12) % 16}
    to_far = {"gz": (gz + 8) % 16}
    step = 1 - 2 * zl
    has_ahead = (xy + step >= 0) & (xy + step < tiles)
    has_behind = (xy - step >= 0) & (xy - step < tiles)
    to_ahead = {"xy": (xy + step + tiles) % tiles}
    to_behind = {"xy": (xy - step + tiles) % tiles}
    partners = (to_core, to_z, to_right, to_left, to_far)
    barrier = pltpu.get_barrier_semaphore()

    def greet(partner):
        pl.semaphore_signal(barrier, inc=1, device_id=partner, device_id_type=MESH)

    for partner in partners:
        greet(partner)
    pl.when(has_ahead)(lambda: greet(to_ahead))
    pl.when(has_behind)(lambda: greet(to_behind))
    greetings = len(partners) + has_ahead.astype(jnp.int32) + has_behind.astype(jnp.int32)

    k_own = zl * 2 + c
    meas_hbm = meas.at[X, pl.ds(pl.multiple_of(8 * k_own, 8), 8)]
    start_copies = [
        pltpu.make_async_copy(ray_hbm, ray, local_sem.at[5]),
        pltpu.make_async_copy(vol_hbm, vol, local_sem.at[6]),
    ]
    for copy in start_copies:
        copy.start()

    @pl.when(jnp.logical_not(has_behind))
    def _():
        halo_g[...] = jnp.zeros_like(halo_g)

    @pl.when(jnp.logical_not(has_ahead))
    def _():
        halo_o[...] = jnp.zeros_like(halo_o)
        meas_rows[1] = jnp.zeros((8, LINE), f32)

    locals_ = [
        pltpu.make_async_copy(defocus_hbm, defocus, local_sem.at[7]),
        pltpu.make_async_copy(line_hbm, line, local_sem.at[8]),
        pltpu.make_async_copy(meas_hbm, meas_rows.at[0], local_sem.at[0]),
        pltpu.make_async_copy(fwd_big_hbm, fwd_big, local_sem.at[1]),
        pltpu.make_async_copy(fwd_small_hbm, fwd_small, local_sem.at[2]),
        pltpu.make_async_copy(inv_big_hbm, inv_big, local_sem.at[3]),
        pltpu.make_async_copy(inv_small_hbm, inv_small, local_sem.at[4]),
    ]
    for copy in locals_:
        copy.start()

    count = [0]
    sent = []
    halos = []

    def send(src, dst, where):
        i = count[0]
        count[0] += 1
        copy = pltpu.make_async_remote_copy(
            src_ref=src, dst_ref=dst, send_sem=ss.at[i], recv_sem=rs.at[i],
            device_id=where, device_id_type=MESH,
        )
        copy.start()
        sent.append(copy)
        return copy

    start_copies[0].wait()
    def send_halo(src, dst, where, there, back):
        i = count[0]
        count[0] += 1
        copy = pltpu.make_async_remote_copy(
            src_ref=src, dst_ref=dst, send_sem=ss.at[i], recv_sem=rs.at[i],
            device_id=where, device_id_type=MESH,
        )
        pl.when(there)(copy.start)
        halos.append((copy, there))
        return lambda: pl.when(back)(copy.wait_recv)

    shift, far = {}, {}
    for dt in range(4):
        t = (X + dt) % 4
        for z in range(LAYERS):
            offset = ray[t, gz * LAYERS + z]
            shift[dt, z] = offset >> 3
            far[dt, z] = (offset & 7).astype(f32) * 0.125

    col = lax.broadcasted_iota(jnp.int32, (8, 128), 1)
    sub = lax.broadcasted_iota(jnp.int32, (8, 128), 0)
    layer = col // ROWS
    target, near_row, far_row = {}, {}, {}
    for dt in range(4):
        s = jnp.zeros((8, 128), jnp.int32)
        w = jnp.zeros((8, 128), f32)
        for z in range(LAYERS):
            s = jnp.where(layer == z, shift[dt, z], s)
            w = jnp.where(layer == z, far[dt, z], w)
        target[dt] = col % ROWS - s
        near_row[dt], far_row[dt] = 1.0 - w, w

    def first_ext(zone, core, ghost):
        base = 8 * (zone * 2 + core)
        if ghost:
            base = base + 32 - 64 * zone
        return base

    def weights(core, ghost, dt, dzl):
        zone = zl ^ dzl
        e = sub + first_ext(zone, core, ghost)
        return jnp.where(e == target[dt], near_row[dt], 0.0) + jnp.where(
            e == target[dt] - 1, far_row[dt], 0.0
        )

    def lhs(core):
        blocks = [weights(core, True, dt, dzl) for dt in range(4) for dzl in range(2)]
        blocks += [weights(core, False, dt, dzl) for dzl in range(2) for dt in range(4)]
        w = jnp.concatenate(blocks, 0).astype(bf16)
        return jnp.concatenate([w, w], 1)

    start_copies[1].wait()
    volume = vol[...].reshape(LAYERS * ROWS, LINE)
    vh, vl = split(volume)
    vcat[0:128, :] = vh
    vcat[128:256, :] = vl

    def project(core, to_g, to_o):
        w = lhs(core)
        for j in range(4):
            at = pl.ds(512 * j, 512)
            p = dot(w, vcat[:, at])
            to_g[:, :, :, at] = p[0:64].reshape(4, 2, 8, 512)
            to_o[:, :, :, at] = p[64:128].reshape(2, 4, 8, 512)

    project(1 - c, other_g, other_o)
    pl.semaphore_wait(barrier, greetings)
    cg, co = {}, {}
    cg[2] = send(other_g.at[2], core_g.at[2], to_core)
    co[1] = send(other_o.at[1], core_o.at[1], to_core)
    cg[1] = send(other_g.at[1], core_g.at[1], to_core)
    cg[3] = send(other_g.at[3], core_g.at[3], to_core)
    co[0] = send(other_o.at[0], core_o.at[0], to_core)
    cg[0] = send(other_g.at[0], core_g.at[0], to_core)
    meas_wait = send_halo(meas_hbm, meas_rows.at[1], to_behind, has_behind, has_ahead)
    project(c, mine_g, mine_o)

    for copy in locals_[:2]:
        copy.wait()
    tilt_row = lax.broadcasted_iota(jnp.int32, (TILTS, 1), 0)
    number = jnp.zeros((TILTS, 1), f32)
    for dt in range(4):
        number = jnp.where(tilt_row == dt, defocus[(X + dt) % 4, gz].astype(f32), number)
    frequency = line[0:1, :]
    phase = math.pi * wavelength * number * frequency * frequency
    response[...] = (
        -(amplitude_root * jnp.sin(phase) + contrast * jnp.cos(phase)) * line[1:2, :]
    )

    gcol = lax.broadcasted_iota(jnp.int32, (ROWS, 256), 1)
    grow = lax.broadcasted_iota(jnp.int32, (ROWS, 256), 0)
    zone = zl ^ ((gcol >> 4) & 1)
    place = 8 * (zone * 2 + (c ^ (gcol >> 7))) + (gcol & 7)
    place = place + ((gcol >> 3) & 1) * (32 - 64 * zone)
    tilt = (gcol >> 5) & 3
    there = place + xy * ROWS
    legal = (there >= 0) & (there < tiles * ROWS)
    back = []
    for z in range(LAYERS):
        s = jnp.zeros((ROWS, 256), jnp.int32)
        w = jnp.zeros((ROWS, 256), f32)
        for dt in range(4):
            s = jnp.where(tilt == dt, shift[dt, z], s)
            w = jnp.where(tilt == dt, far[dt, z], w)
        delta = place + s - grow
        both = jnp.where(delta == 0, 1.0 - w, 0.0) + jnp.where(delta == -1, w, 0.0)
        back.append(jnp.where(legal, both, 0.0))
    back_rows[...] = jnp.concatenate(back, 0).astype(bf16)

    def add(dst, src):
        dst[...] = dst[...] + src[...]

    cg[2].wait_recv()
    add(mine_g.at[2], core_g.at[2])
    g_far = send(mine_g.at[2], fin_g.at[2], to_far)
    co[1].wait_recv()
    add(mine_o.at[1], core_o.at[1])
    oz = {}
    for dt in (2, 1, 3, 0):
        oz[dt] = send(mine_o.at[1, dt], zin_o.at[dt], to_z)
    cg[1].wait_recv()
    add(mine_g.at[1], core_g.at[1])
    g_right = send(mine_g.at[1], fin_g.at[0], to_right)
    cg[3].wait_recv()
    add(mine_g.at[3], core_g.at[3])
    g_left = send(mine_g.at[3], fin_g.at[1], to_left)
    co[0].wait_recv()
    add(mine_o.at[0], core_o.at[0])
    cg[0].wait_recv()
    add(mine_g.at[0], core_g.at[0])

    oz[2].wait_recv()
    add(mine_o.at[0, 2], zin_o.at[2])
    o_far = send(mine_o.at[0, 2], fin_o.at[2], to_far)
    oz[1].wait_recv()
    add(mine_o.at[0, 1], zin_o.at[1])
    o_right = send(mine_o.at[0, 1], fin_o.at[0], to_right)
    oz[3].wait_recv()
    add(mine_o.at[0, 3], zin_o.at[3])
    o_left = send(mine_o.at[0, 3], fin_o.at[1], to_left)

    g_far.wait_recv()
    g_right.wait_recv()
    g_left.wait_recv()
    mine_g[0] = (mine_g[0] + fin_g[0]) + (fin_g[1] + fin_g[2])
    g_z = send(mine_g.at[0, 1], zin_g, to_z)

    oz[0].wait_recv()
    o_far.wait_recv()
    o_right.wait_recv()
    o_left.wait_recv()
    mine_o[0, 0] = (mine_o[0, 0] + zin_o[0]) + (fin_o[0] + fin_o[1]) + fin_o[2]
    o_wait = send_halo(mine_o.at[0, 0], halo_o, to_behind, has_behind, has_ahead)
    g_z.wait_recv()
    add(mine_g.at[0, 0], zin_g)
    g_wait = send_halo(mine_g.at[0, 0], halo_g, to_ahead, has_ahead, has_behind)
    for copy in locals_[2:]:
        copy.wait()

    g_wait()
    o_wait()
    meas_wait()
    ray_norm = float(TILTS * 16) ** (-0.5)
    own_sum = mine_o[0, 0] + jnp.where(has_behind, halo_g[...], 0.0)
    own_rows = meas_rows[0] - ray_norm * own_sum
    ghost_rows = meas_rows[1] - ray_norm * (mine_g[0, 0] + halo_o[...])
    ghost_rows = jnp.where(has_ahead, ghost_rows, 0.0)
    residual = jnp.concatenate([own_rows, ghost_rows], 0)

    x = [residual[:, PART * a : PART * (a + 1)] for a in range(8)]
    root = math.sqrt(0.5)
    s04, d04 = x[0] + x[4], x[0] - x[4]
    s26, d26 = x[2] + x[6], x[2] - x[6]
    s15, d15 = x[1] + x[5], x[1] - x[5]
    s37, d37 = x[3] + x[7], x[3] - x[7]
    even, odd = s04 + s26, s15 + s37
    m = root * (d15 - d37)
    n = root * (d15 + d37)
    inputs = {
        0: even + odd,
        4: even - odd,
        1: jnp.concatenate([d04 + m, -(d26 + n)], 1),
        2: jnp.concatenate([s04 - s26, s37 - s15], 1),
        3: jnp.concatenate([d04 - m, d26 - n], 1),
    }
    for first, width, residue in GROUPS:
        high, low = split(inputs[residue])
        if width == 512:
            th, tl = fwd_big[0, residue - 1], fwd_big[1, residue - 1]
        else:
            th, tl = fwd_small[0, residue // 4], fwd_small[1, residue // 4]
        both = dot(jnp.concatenate([high, low], 0), th)
        lines = both[0:16] + both[16:32] + dot(high, tl)
        gathered[0, 0, 0, :, :, first : first + width] = lines.reshape(2, 8, width)

    def block(dt, dzl, ghost):
        return gathered.at[0, dt, dzl, ghost]

    def along_x(dzl, ghost):
        src = block(0, dzl, ghost)
        far = send(src, block(2, dzl, ghost), to_far)
        right = send(src, block(3, dzl, ghost), to_right)
        left = send(src, block(1, dzl, ghost), to_left)
        return {2: far, 3: right, 1: left}

    def along_z(dt, ghost):
        return send(block(dt, 0, ghost), block(dt, 1, ghost), to_z)

    cores = []

    def to_other(dt, dzl, ghost):
        cores.append(send(block(dt, dzl, ghost), gathered.at[1, dt, dzl, ghost], to_core))

    gz0 = along_z(0, 1)
    ox = along_x(0, 0)
    oz0 = along_z(0, 0)
    gx = along_x(0, 1)
    cores.append(send(gathered.at[0, 0, 0], gathered.at[1, 0, 0], to_core))
    gz0.wait_recv()
    gzx = along_x(1, 1)
    to_other(0, 1, 1)
    ozs = {}
    for dt in (3, 1, 2):
        ox[dt].wait_recv()
        ozs[dt] = along_z(dt, 0)
        to_other(dt, 0, 0)
    oz0.wait_recv()
    to_other(0, 1, 0)
    for dt in (3, 1, 2):
        gx[dt].wait_recv()
        to_other(dt, 0, 1)
    for dt in (3, 1, 2):
        ozs[dt].wait_recv()
        to_other(dt, 1, 0)
        gzx[dt].wait_recv()
        to_other(dt, 1, 1)
    for copy in cores:
        copy.wait_recv()

    for first, width, residue in GROUPS:
        at = pl.ds(first, width)
        highs, lows = [], []
        for dc in range(2):
            for dt in range(4):
                lines = gathered[dc, dt, :, :, :, at].reshape(32, width)
                high, low = split(lines * response[dt : dt + 1, at])
                highs.append(high)
                lows.append(low)
        back = back_rows[...]
        u = dot(back, jnp.concatenate(highs, 0)) + dot(back, jnp.concatenate(lows, 0))
        high, low = split(u)
        if width == 512:
            th, tl = inv_big[0, residue - 1], inv_big[1, residue - 1]
        else:
            th, tl = inv_small[0, residue // 4], inv_small[1, residue // 4]
        spectral[:, at] = dot(high, th) + dot(low, th) + dot(high, tl)

    def part(first):
        return spectral[:, first : first + PART]

    g0, g4 = part(0), part(256)
    r1, i1, r2, i2, r3, i3 = (part(512 + PART * i) for i in range(6))
    p, q = g0 + g4, g0 - g4
    pr, ps = p + r2, p - r2
    qm, qp = q - i2, q + i2
    r13, i31 = r1 + r3, i3 - i1
    rd, im = r1 - r3, i1 + i3
    v, w = root * (rd - im), root * (rd + im)
    ys = (pr + r13, qm + v, ps + i31, qp - w, pr - r13, qm - v, ps - i31, qp + w)
    for a in range(8):
        at = pl.ds(PART * a, PART)
        out[:, :, at] = vol[:, :, at] + ys[a].reshape(LAYERS, ROWS, PART)

    for copy in sent:
        copy.wait_send()
    for copy, there in halos:
        pl.when(there)(copy.wait_send)


def body(tiles, tables, volume, measured, ray_offset, defocus):
    fwd_big, fwd_small, inv_big, inv_small, line = tables
    hbm = pl.BlockSpec(memory_space=pltpu.HBM)

    def f(*shape):
        return pltpu.VMEM(shape, f32)

    return pl.pallas_call(
        functools.partial(kernel, tiles),
        out_shape=jax.ShapeDtypeStruct(volume.shape, f32),
        in_specs=[hbm] * 9,
        out_specs=pl.BlockSpec(memory_space=pltpu.VMEM),
        scratch_shapes=[
            pltpu.SMEM(ray_offset.shape, jnp.int32),
            pltpu.SMEM(defocus.shape, jnp.int32),
            f(*volume.shape),
            f(*line.shape),
            f(TILTS, LINE),
            pltpu.VMEM((128, 256), bf16),
            pltpu.VMEM(fwd_big.shape, bf16),
            pltpu.VMEM(fwd_small.shape, bf16),
            pltpu.VMEM(inv_big.shape, bf16),
            pltpu.VMEM(inv_small.shape, bf16),
            f(2, 8, LINE),
            pltpu.VMEM((256, LINE), bf16),
            f(4, 2, 8, LINE),
            f(2, 4, 8, LINE),
            f(4, 2, 8, LINE),
            f(2, 4, 8, LINE),
            f(4, 2, 8, LINE),
            f(2, 4, 8, LINE),
            f(3, 2, 8, LINE),
            f(8, LINE),
            f(4, 8, LINE),
            f(3, 8, LINE),
            f(8, LINE),
            f(8, LINE),
            f(2, 4, 2, 2, 8, LINE),
            f(128, LINE),
            pltpu.SemaphoreType.DMA((9,)),
            pltpu.SemaphoreType.DMA((64,)),
            pltpu.SemaphoreType.DMA((64,)),
        ],
        compiler_params=pltpu.CompilerParams(
            collective_id=0, has_side_effects=True, vmem_limit_bytes=60 * 1024 * 1024
        ),
        name="step",
    )(ray_offset, defocus, volume, measured, line, fwd_big, fwd_small, inv_big, inv_small)


def solution(mesh):
    placed = (P("gz", "xy", None), P(None, "xy", None), P(), P())
    tables = tuple(dft_tables())
    return jax.shard_map(
        functools.partial(body, mesh.shape["xy"], tables),
        mesh=mesh,
        in_specs=placed,
        out_specs=P("gz", "xy", None),
        check_vma=False,
    )
```

time: 61.5 us -> 43.6 us (0.71)
  the two profiles are of different devices: /device:TPU:1 before, /device:TPU:259 now
where the time goes in v2:
time: 43.6 us; the launch traced here: 43.5 us
  Pallas kernels  41.2 us (94%)
  local copies, waits for them, and re-layouts  2.3 us (5%)
    pallas_call x1, Pallas kernels, body(): pl.pallas_call(functools.partial(kernel, tiles), out_shape=jax.ShapeDtype...  41.2 us
    unnamed x1, local copies, waits for them, and re-layouts  2.3 us

profile of v2, /device:TPU:259, one launch (start us, length us, event | category | flops | bytes accessed | tf_op | source)
XLA Modules:
  0.0 43.5 jit_solution(13793625712929070388)
XLA Ops:
  0.0 41.2 %step.1 = f32[4,32,2048]{2,1,0:T(8,128)} custom-call(s32[4,64]{1,0:T(4,128)} %ray_hbm.1, s32[4,16]{1,0:T(4,128)} %defocus_hbm.1, f32[4,32,2048]{2,1,0:T(8,128)} %vol_hbm.1, f32[4,32,2048]{2,1,0:T(8,128)} %meas.1, f32[2,2048]{1,0:T(2,128)} %constant.10.clone.line_hbm, bf16[2,3,512,512]{3,2,1,0:T(8,128)(2,1)} %constant.11.clone.fwd_big_hbm, ...), custom_call_target="tpu_custom_call" | custom-call | tf_op jit(solution)/shard_map/step/pallas_call | solution.py:482
  41.2 2.3 %copy.11 = f32[4,32,2048]{2,1,0:T(8,128)} copy(f32[4,32,2048]{2,1,0:T(8,128)} %step.1) | data formatting | bytes 2097152

commit v3 on v2

--- a/solution.py
+++ b/solution.py
@@ -16,6 +16,9 @@
 ROWS = 32
 LAYERS = 4
 TILTS = 4
+SUM_PARTS = 2
+SEMAPHORES = 64
+GATHER_PARTS = 1
 
 pixel_size = 4.0
 wavelength = 0.0197
@@ -116,6 +119,7 @@
     halo_o,
     gathered,
     spectral,
+    terms,
     local_sem,
     ss,
     rs,
@@ -149,9 +153,10 @@
 
     k_own = zl * 2 + c
     meas_hbm = meas.at[X, pl.ds(pl.multiple_of(8 * k_own, 8), 8)]
-    start_copies = [
-        pltpu.make_async_copy(ray_hbm, ray, local_sem.at[5]),
-        pltpu.make_async_copy(vol_hbm, vol, local_sem.at[6]),
+    quarter = [pl.ds(512 * j, 512) for j in range(4)]
+    start_copies = [pltpu.make_async_copy(ray_hbm, ray, local_sem.at[5])] + [
+        pltpu.make_async_copy(vol_hbm.at[:, :, quarter[j]], vol.at[:, :, quarter[j]], local_sem.at[8 + j])
+        for j in range(4)
     ]
     for copy in start_copies:
         copy.start()
@@ -167,16 +172,13 @@
 
     locals_ = [
         pltpu.make_async_copy(defocus_hbm, defocus, local_sem.at[7]),
-        pltpu.make_async_copy(line_hbm, line, local_sem.at[8]),
+        pltpu.make_async_copy(line_hbm, line, local_sem.at[6]),
         pltpu.make_async_copy(meas_hbm, meas_rows.at[0], local_sem.at[0]),
         pltpu.make_async_copy(fwd_big_hbm, fwd_big, local_sem.at[1]),
         pltpu.make_async_copy(fwd_small_hbm, fwd_small, local_sem.at[2]),
         pltpu.make_async_copy(inv_big_hbm, inv_big, local_sem.at[3]),
         pltpu.make_async_copy(inv_small_hbm, inv_small, local_sem.at[4]),
     ]
-    for copy in locals_:
-        copy.start()
-
     count = [0]
     sent = []
     halos = []
@@ -244,21 +246,19 @@
         w = jnp.concatenate(blocks, 0).astype(bf16)
         return jnp.concatenate([w, w], 1)
 
-    start_copies[1].wait()
-    volume = vol[...].reshape(LAYERS * ROWS, LINE)
-    vh, vl = split(volume)
-    vcat[0:128, :] = vh
-    vcat[128:256, :] = vl
-
-    def project(core, to_g, to_o):
+    def project(core, to_g, to_o, fill=False):
         w = lhs(core)
-        for j in range(4):
-            at = pl.ds(512 * j, 512)
+        for j, at in enumerate(quarter):
+            if fill:
+                start_copies[1 + j].wait()
+                high, low = split(vol[:, :, at].reshape(LAYERS * ROWS, 512))
+                vcat[0:128, at] = high
+                vcat[128:256, at] = low
             p = dot(w, vcat[:, at])
             to_g[:, :, :, at] = p[0:64].reshape(4, 2, 8, 512)
             to_o[:, :, :, at] = p[64:128].reshape(2, 4, 8, 512)
 
-    project(1 - c, other_g, other_o)
+    project(1 - c, other_g, other_o, fill=True)
     pl.semaphore_wait(barrier, greetings)
     cg, co = {}, {}
     cg[2] = send(other_g.at[2], core_g.at[2], to_core)
@@ -267,8 +267,37 @@
     cg[3] = send(other_g.at[3], core_g.at[3], to_core)
     co[0] = send(other_o.at[0], core_o.at[0], to_core)
     cg[0] = send(other_g.at[0], core_g.at[0], to_core)
+    for copy in locals_:
+        copy.start()
     meas_wait = send_halo(meas_hbm, meas_rows.at[1], to_behind, has_behind, has_ahead)
     project(c, mine_g, mine_o)
+
+    def add(dst, src):
+        dst[...] = dst[...] + src[...]
+
+    width = LINE // SUM_PARTS
+    parts = [pl.ds(width * i, width) for i in range(SUM_PARTS)]
+    cg[2].wait_recv()
+    add(mine_g.at[2], core_g.at[2])
+    gx, ox, oz = {}, {}, {}
+    for i, at in enumerate(parts):
+        gx[2, i] = send(mine_g.at[2, :, :, at], fin_g.at[2, :, :, at], to_far)
+    co[1].wait_recv()
+    add(mine_o.at[1], core_o.at[1])
+    for i, at in enumerate(parts):
+        for dt in (2, 1, 3, 0):
+            oz[dt, i] = send(mine_o.at[1, dt, :, at], zin_o.at[dt, :, at], to_z)
+    cg[1].wait_recv()
+    add(mine_g.at[1], core_g.at[1])
+    cg[3].wait_recv()
+    add(mine_g.at[3], core_g.at[3])
+    for i, at in enumerate(parts):
+        gx[1, i] = send(mine_g.at[1, :, :, at], fin_g.at[0, :, :, at], to_right)
+        gx[3, i] = send(mine_g.at[3, :, :, at], fin_g.at[1, :, :, at], to_left)
+    co[0].wait_recv()
+    add(mine_o.at[0], core_o.at[0])
+    cg[0].wait_recv()
+    add(mine_g.at[0], core_g.at[0])
 
     for copy in locals_[:2]:
         copy.wait()
@@ -302,59 +331,42 @@
         back.append(jnp.where(legal, both, 0.0))
     back_rows[...] = jnp.concatenate(back, 0).astype(bf16)
 
-    def add(dst, src):
-        dst[...] = dst[...] + src[...]
-
-    cg[2].wait_recv()
-    add(mine_g.at[2], core_g.at[2])
-    g_far = send(mine_g.at[2], fin_g.at[2], to_far)
-    co[1].wait_recv()
-    add(mine_o.at[1], core_o.at[1])
-    oz = {}
-    for dt in (2, 1, 3, 0):
-        oz[dt] = send(mine_o.at[1, dt], zin_o.at[dt], to_z)
-    cg[1].wait_recv()
-    add(mine_g.at[1], core_g.at[1])
-    g_right = send(mine_g.at[1], fin_g.at[0], to_right)
-    cg[3].wait_recv()
-    add(mine_g.at[3], core_g.at[3])
-    g_left = send(mine_g.at[3], fin_g.at[1], to_left)
-    co[0].wait_recv()
-    add(mine_o.at[0], core_o.at[0])
-    cg[0].wait_recv()
-    add(mine_g.at[0], core_g.at[0])
-
-    oz[2].wait_recv()
-    add(mine_o.at[0, 2], zin_o.at[2])
-    o_far = send(mine_o.at[0, 2], fin_o.at[2], to_far)
-    oz[1].wait_recv()
-    add(mine_o.at[0, 1], zin_o.at[1])
-    o_right = send(mine_o.at[0, 1], fin_o.at[0], to_right)
-    oz[3].wait_recv()
-    add(mine_o.at[0, 3], zin_o.at[3])
-    o_left = send(mine_o.at[0, 3], fin_o.at[1], to_left)
-
-    g_far.wait_recv()
-    g_right.wait_recv()
-    g_left.wait_recv()
-    mine_g[0] = (mine_g[0] + fin_g[0]) + (fin_g[1] + fin_g[2])
-    g_z = send(mine_g.at[0, 1], zin_g, to_z)
-
-    oz[0].wait_recv()
-    o_far.wait_recv()
-    o_right.wait_recv()
-    o_left.wait_recv()
-    mine_o[0, 0] = (mine_o[0, 0] + zin_o[0]) + (fin_o[0] + fin_o[1]) + fin_o[2]
-    o_wait = send_halo(mine_o.at[0, 0], halo_o, to_behind, has_behind, has_ahead)
-    g_z.wait_recv()
-    add(mine_g.at[0, 0], zin_g)
-    g_wait = send_halo(mine_g.at[0, 0], halo_g, to_ahead, has_ahead, has_behind)
+    gz_, waits = {}, []
+    for i, at in enumerate(parts):
+        for dt, slot, where in ((2, 2, to_far), (1, 0, to_right), (3, 1, to_left)):
+            oz[dt, i].wait_recv()
+            add(mine_o.at[0, dt, :, at], zin_o.at[dt, :, at])
+            ox[dt, i] = send(mine_o.at[0, dt, :, at], fin_o.at[slot, :, at], where)
+    for i, at in enumerate(parts):
+        for dt in (2, 1, 3):
+            gx[dt, i].wait_recv()
+        mine_g[0, :, :, at] = (mine_g[0, :, :, at] + fin_g[0, :, :, at]) + (
+            fin_g[1, :, :, at] + fin_g[2, :, :, at]
+        )
+        gz_[i] = send(mine_g.at[0, 1, :, at], zin_g.at[:, at], to_z)
+    for i, at in enumerate(parts):
+        oz[0, i].wait_recv()
+        for dt in (2, 1, 3):
+            ox[dt, i].wait_recv()
+        mine_o[0, 0, :, at] = (
+            (mine_o[0, 0, :, at] + zin_o[0, :, at])
+            + (fin_o[0, :, at] + fin_o[1, :, at])
+            + fin_o[2, :, at]
+        )
+        waits.append(
+            send_halo(mine_o.at[0, 0, :, at], halo_o.at[:, at], to_behind, has_behind, has_ahead)
+        )
+        gz_[i].wait_recv()
+        add(mine_g.at[0, 0, :, at], zin_g.at[:, at])
+        waits.append(
+            send_halo(mine_g.at[0, 0, :, at], halo_g.at[:, at], to_ahead, has_ahead, has_behind)
+        )
     for copy in locals_[2:]:
         copy.wait()
 
-    g_wait()
-    o_wait()
     meas_wait()
+    for wait in waits:
+        wait()
     ray_norm = float(TILTS * 16) ** (-0.5)
     own_sum = mine_o[0, 0] + jnp.where(has_behind, halo_g[...], 0.0)
     own_rows = meas_rows[0] - ray_norm * own_sum
@@ -388,62 +400,95 @@
         lines = both[0:16] + both[16:32] + dot(high, tl)
         gathered[0, 0, 0, :, :, first : first + width] = lines.reshape(2, 8, width)
 
-    def block(dt, dzl, ghost):
-        return gathered.at[0, dt, dzl, ghost]
-
-    def along_x(dzl, ghost):
-        src = block(0, dzl, ghost)
-        far = send(src, block(2, dzl, ghost), to_far)
-        right = send(src, block(3, dzl, ghost), to_right)
-        left = send(src, block(1, dzl, ghost), to_left)
-        return {2: far, 3: right, 1: left}
-
-    def along_z(dt, ghost):
-        return send(block(dt, 0, ghost), block(dt, 1, ghost), to_z)
-
-    cores = []
-
-    def to_other(dt, dzl, ghost):
-        cores.append(send(block(dt, dzl, ghost), gathered.at[1, dt, dzl, ghost], to_core))
-
-    gz0 = along_z(0, 1)
-    ox = along_x(0, 0)
-    oz0 = along_z(0, 0)
-    gx = along_x(0, 1)
-    cores.append(send(gathered.at[0, 0, 0], gathered.at[1, 0, 0], to_core))
-    gz0.wait_recv()
-    gzx = along_x(1, 1)
-    to_other(0, 1, 1)
-    ozs = {}
+    piece = LINE // GATHER_PARTS
+    pieces = [pl.ds(piece * i, piece) for i in range(GATHER_PARTS)]
+
+    def block(dt, dzl, ghost, i):
+        return gathered.at[0, dt, dzl, ghost, :, pieces[i]]
+
+    def along_x(dzl, ghost, i):
+        src = block(0, dzl, ghost, i)
+        return {
+            2: send(src, block(2, dzl, ghost, i), to_far),
+            3: send(src, block(3, dzl, ghost, i), to_right),
+            1: send(src, block(1, dzl, ghost, i), to_left),
+        }
+
+    def along_z(dt, ghost, i):
+        return send(block(dt, 0, ghost, i), block(dt, 1, ghost, i), to_z)
+
+    passed = {}
+
+    def to_other(dt, dzl, ghost, i):
+        src = block(dt, dzl, ghost, i)
+        passed.setdefault((dt, dzl), []).append(
+            send(src, gathered.at[1, dt, dzl, ghost, :, pieces[i]], to_core)
+        )
+
+    def scale(core, dt, dzl):
+        lines = gathered[core, dt, dzl].reshape(16, LINE) * response[dt : dt + 1, :]
+        high, low = split(lines)
+        first = 256 * core + 32 * dt + 16 * dzl
+        terms[first : first + 16, :] = high
+        terms[first + 128 : first + 144, :] = low
+
+    def combine(core):
+        w = back_rows[:, 128 * core : 128 * core + 128]
+        w = jnp.concatenate([w, w], 1)
+        for at in quarter:
+            u = dot(w, terms[256 * core : 256 * core + 256, at])
+            spectral[:, at] = spectral[:, at] + u if core else u
+
+    n = range(GATHER_PARTS)
+    az, bx, bz, cx, cz = {}, {}, {}, {}, {}
+    for i in n:
+        az[i] = along_z(0, 1, i)
+        bx[i] = along_x(0, 0, i)
+        bz[0, i] = along_z(0, 0, i)
+    for i in n:
+        cx[i] = along_x(0, 1, i)
+    for i in n:
+        to_other(0, 0, 0, i)
+        to_other(0, 0, 1, i)
+    for i in n:
+        az[i].wait_recv()
+        cz[i] = along_x(1, 1, i)
+        to_other(0, 1, 1, i)
+    for i in n:
+        for dt in (3, 1, 2):
+            bx[i][dt].wait_recv()
+            bz[dt, i] = along_z(dt, 0, i)
+            to_other(dt, 0, 0, i)
+    scale(0, 0, 0)
+    for i in n:
+        bz[0, i].wait_recv()
+        to_other(0, 1, 0, i)
+    scale(0, 0, 1)
     for dt in (3, 1, 2):
-        ox[dt].wait_recv()
-        ozs[dt] = along_z(dt, 0)
-        to_other(dt, 0, 0)
-    oz0.wait_recv()
-    to_other(0, 1, 0)
+        for i in n:
+            cx[i][dt].wait_recv()
+            to_other(dt, 0, 1, i)
+        scale(0, dt, 0)
+    for copy in passed[0, 0]:
+        copy.wait_recv()
+    scale(1, 0, 0)
     for dt in (3, 1, 2):
-        gx[dt].wait_recv()
-        to_other(dt, 0, 1)
-    for dt in (3, 1, 2):
-        ozs[dt].wait_recv()
-        to_other(dt, 1, 0)
-        gzx[dt].wait_recv()
-        to_other(dt, 1, 1)
-    for copy in cores:
-        copy.wait_recv()
+        for i in n:
+            bz[dt, i].wait_recv()
+            to_other(dt, 1, 0, i)
+            cz[i][dt].wait_recv()
+            to_other(dt, 1, 1, i)
+        scale(0, dt, 1)
+    combine(0)
+    for key in ((0, 1), (3, 0), (1, 0), (2, 0), (3, 1), (1, 1), (2, 1)):
+        for copy in passed[key]:
+            copy.wait_recv()
+        scale(1, *key)
+    combine(1)
 
     for first, width, residue in GROUPS:
         at = pl.ds(first, width)
-        highs, lows = [], []
-        for dc in range(2):
-            for dt in range(4):
-                lines = gathered[dc, dt, :, :, :, at].reshape(32, width)
-                high, low = split(lines * response[dt : dt + 1, at])
-                highs.append(high)
-                lows.append(low)
-        back = back_rows[...]
-        u = dot(back, jnp.concatenate(highs, 0)) + dot(back, jnp.concatenate(lows, 0))
-        high, low = split(u)
+        high, low = split(spectral[:, at])
         if width == 512:
             th, tl = inv_big[0, residue - 1], inv_big[1, residue - 1]
         else:
@@ -479,9 +524,10 @@
     def f(*shape):
         return pltpu.VMEM(shape, f32)
 
+    arrays = (ray_offset, defocus, volume, measured, line, fwd_big, fwd_small, inv_big, inv_small)
     return pl.pallas_call(
         functools.partial(kernel, tiles),
-        out_shape=jax.ShapeDtypeStruct(volume.shape, f32),
+        out_shape=pltpu.VMEM(volume.shape, f32),
         in_specs=[hbm] * 9,
         out_specs=pl.BlockSpec(memory_space=pltpu.VMEM),
         scratch_shapes=[
@@ -511,15 +557,16 @@
             f(8, LINE),
             f(2, 4, 2, 2, 8, LINE),
             f(128, LINE),
-            pltpu.SemaphoreType.DMA((9,)),
-            pltpu.SemaphoreType.DMA((64,)),
-            pltpu.SemaphoreType.DMA((64,)),
+            pltpu.VMEM((512, LINE), bf16),
+            pltpu.SemaphoreType.DMA((12,)),
+            pltpu.SemaphoreType.DMA((SEMAPHORES,)),
+            pltpu.SemaphoreType.DMA((SEMAPHORES,)),
         ],
         compiler_params=pltpu.CompilerParams(
-            collective_id=0, has_side_effects=True, vmem_limit_bytes=60 * 1024 * 1024
+            collective_id=0, has_side_effects=True, vmem_limit_bytes=40 * 1024 * 1024
         ),
         name="step",
-    )(ray_offset, defocus, volume, measured, line, fwd_big, fwd_small, inv_big, inv_small)
+    )(*(pltpu.with_memory_space_constraint(a, pltpu.HBM) for a in arrays))
 
 
 def solution(mesh):

time: 43.6 us -> 40.5 us (0.929)
  the two profiles are of different devices: /device:TPU:259 before, /device:TPU:185 now
where the time goes in v3:
time: 40.5 us; the launch traced here: 40.4 us
  Pallas kernels  39.4 us (97%)
  local copies, waits for them, and re-layouts  0.97 us (2%)
    pallas_call x1, Pallas kernels, body(): pl.pallas_call(functools.partial(kernel, tiles), out_shape=pltpu.VMEM(vol...  39.4 us
    unnamed x1, local copies, waits for them, and re-layouts  0.97 us

profile of v3, /device:TPU:185, one launch (start us, length us, event | category | flops | bytes accessed | tf_op | source)
XLA Modules:
  0.0 40.4 jit_solution(5879818568463936417)
XLA Ops:
  0.0 39.4 %step.1 = f32[4,32,2048]{2,1,0:T(8,128)S(1)} custom-call(s32[4,64]{1,0:T(4,128)} %ray_hbm.1, s32[4,16]{1,0:T(4,128)} %defocus_hbm.1, f32[4,32,2048]{2,1,0:T(8,128)} %vol_hbm.1, f32[4,32,2048]{2,1,0:T(8,128)} %meas.1, f32[2,2048]{1,0:T(2,128)} %constant.10.clone.line_hbm, bf16[2,3,512,512]{3,2,1,0:T(8,128)(2,1)} %constant.11.clone.fwd_big_hbm, ...), custom_call_target="tpu_custom_call" | custom-call | tf_op jit(solution)/shard_map/step/pallas_call | solution.py:528
  39.4 1.0 %copy.11 = f32[4,32,2048]{2,1,0:T(8,128)} copy(f32[4,32,2048]{2,1,0:T(8,128)S(1)} %step.1) | data formatting | bytes 2097152

commit v4 on v3

--- a/solution.py
+++ b/solution.py
@@ -18,7 +18,6 @@
 TILTS = 4
 SUM_PARTS = 2
 SEMAPHORES = 64
-GATHER_PARTS = 1
 
 pixel_size = 4.0
 wavelength = 0.0197
@@ -400,29 +399,32 @@
         lines = both[0:16] + both[16:32] + dot(high, tl)
         gathered[0, 0, 0, :, :, first : first + width] = lines.reshape(2, 8, width)
 
-    piece = LINE // GATHER_PARTS
-    pieces = [pl.ds(piece * i, piece) for i in range(GATHER_PARTS)]
-
-    def block(dt, dzl, ghost, i):
-        return gathered.at[0, dt, dzl, ghost, :, pieces[i]]
-
-    def along_x(dzl, ghost, i):
-        src = block(0, dzl, ghost, i)
+    half = (pl.ds(0, LINE // 2), pl.ds(LINE // 2, LINE // 2))
+
+    def block(dt, dzl, ghost):
+        return gathered.at[0, dt, dzl, ghost]
+
+    def to_sides(dzl, ghost):
+        src = block(0, dzl, ghost)
         return {
-            2: send(src, block(2, dzl, ghost, i), to_far),
-            3: send(src, block(3, dzl, ghost, i), to_right),
-            1: send(src, block(1, dzl, ghost, i), to_left),
+            3: send(src, block(3, dzl, ghost), to_right),
+            1: send(src, block(1, dzl, ghost), to_left),
         }
 
-    def along_z(dt, ghost, i):
-        return send(block(dt, 0, ghost, i), block(dt, 1, ghost, i), to_z)
+    def pass_on(dt, dzl, ghost):
+        at, where = (half[0], to_right) if dt == 3 else (half[1], to_left)
+        src = gathered.at[0, dt, dzl, ghost, :, at]
+        return send(src, gathered.at[0, 2, dzl, ghost, :, at], where)
+
+    def along_z(dt, ghost):
+        return send(block(dt, 0, ghost), block(dt, 1, ghost), to_z)
 
     passed = {}
 
-    def to_other(dt, dzl, ghost, i):
-        src = block(dt, dzl, ghost, i)
+    def to_other(dt, dzl, ghost):
+        src = block(dt, dzl, ghost)
         passed.setdefault((dt, dzl), []).append(
-            send(src, gathered.at[1, dt, dzl, ghost, :, pieces[i]], to_core)
+            send(src, gathered.at[1, dt, dzl, ghost], to_core)
         )
 
     def scale(core, dt, dzl):
@@ -439,48 +441,58 @@
             u = dot(w, terms[256 * core : 256 * core + 256, at])
             spectral[:, at] = spectral[:, at] + u if core else u
 
-    n = range(GATHER_PARTS)
-    az, bx, bz, cx, cz = {}, {}, {}, {}, {}
-    for i in n:
-        az[i] = along_z(0, 1, i)
-        bx[i] = along_x(0, 0, i)
-        bz[0, i] = along_z(0, 0, i)
-    for i in n:
-        cx[i] = along_x(0, 1, i)
-    for i in n:
-        to_other(0, 0, 0, i)
-        to_other(0, 0, 1, i)
-    for i in n:
-        az[i].wait_recv()
-        cz[i] = along_x(1, 1, i)
-        to_other(0, 1, 1, i)
-    for i in n:
-        for dt in (3, 1, 2):
-            bx[i][dt].wait_recv()
-            bz[dt, i] = along_z(dt, 0, i)
-            to_other(dt, 0, 0, i)
+    bx = to_sides(0, 0)
+    az = along_z(0, 1)
+    bx[2] = send(block(0, 0, 0), block(2, 0, 0), to_far)
+    bz = {0: along_z(0, 0)}
+    cx = to_sides(0, 1)
+    to_other(0, 0, 0)
+    to_other(0, 0, 1)
+    for dt in (3, 1):
+        bx[dt].wait_recv()
+        bz[dt] = along_z(dt, 0)
+    az.wait_recv()
+    cz = {2: send(block(0, 1, 1), block(2, 1, 1), to_far)}
+    cz.update(to_sides(1, 1))
+    to_other(0, 1, 1)
+    to_other(3, 0, 0)
+    to_other(1, 0, 0)
+    bz[0].wait_recv()
+    to_other(0, 1, 0)
     scale(0, 0, 0)
-    for i in n:
-        bz[0, i].wait_recv()
-        to_other(0, 1, 0, i)
+    bx[2].wait_recv()
+    bz[2] = along_z(2, 0)
+    cfar = []
+    for dt in (3, 1):
+        cx[dt].wait_recv()
+        cfar.append(pass_on(dt, 0, 1))
+    to_other(2, 0, 0)
+    to_other(3, 0, 1)
+    to_other(1, 0, 1)
     scale(0, 0, 1)
-    for dt in (3, 1, 2):
-        for i in n:
-            cx[i][dt].wait_recv()
-            to_other(dt, 0, 1, i)
+    for dt in (3, 1):
         scale(0, dt, 0)
+    bz[3].wait_recv()
+    to_other(3, 1, 0)
     for copy in passed[0, 0]:
         copy.wait_recv()
     scale(1, 0, 0)
-    for dt in (3, 1, 2):
-        for i in n:
-            bz[dt, i].wait_recv()
-            to_other(dt, 1, 0, i)
-            cz[i][dt].wait_recv()
-            to_other(dt, 1, 1, i)
-        scale(0, dt, 1)
+    bz[1].wait_recv()
+    to_other(1, 1, 0)
+    for dt in (2, 3, 1):
+        cz[dt].wait_recv()
+        to_other(dt, 1, 1)
+    for copy in cfar:
+        copy.wait_recv()
+    to_other(2, 0, 1)
+    scale(0, 2, 0)
+    scale(0, 3, 1)
+    scale(0, 1, 1)
+    bz[2].wait_recv()
+    to_other(2, 1, 0)
+    scale(0, 2, 1)
     combine(0)
-    for key in ((0, 1), (3, 0), (1, 0), (2, 0), (3, 1), (1, 1), (2, 1)):
+    for key in ((0, 1), (3, 0), (1, 0), (3, 1), (1, 1), (2, 0), (2, 1)):
         for copy in passed[key]:
             copy.wait_recv()
         scale(1, *key)

time: 40.5 us -> 39.3 us (0.970)
  Pallas kernels: 39.4 us -> 38.1 us
    pallas_call x1, Pallas kernels: 39.4 us -> 38.1 us  [body(): pl.pallas_call(functools.partial(kernel, tiles), out_shape=pltpu.VMEM(vol...]
where the time goes in v4:
time: 39.3 us; the launch traced here: 39.1 us
  Pallas kernels  38.1 us (97%)
  local copies, waits for them, and re-layouts  0.97 us (2%)
    pallas_call x1, Pallas kernels, body(): pl.pallas_call(functools.partial(kernel, tiles), out_shape=pltpu.VMEM(vol...  38.1 us
    unnamed x1, local copies, waits for them, and re-layouts  0.97 us

profile of v4, /device:TPU:185, one launch (start us, length us, event | category | flops | bytes accessed | tf_op | source)
XLA Modules:
  0.0 39.1 jit_solution(9733641897491999727)
XLA Ops:
  0.0 38.1 %step.1 = f32[4,32,2048]{2,1,0:T(8,128)S(1)} custom-call(s32[4,64]{1,0:T(4,128)} %ray_hbm.1, s32[4,16]{1,0:T(4,128)} %defocus_hbm.1, f32[4,32,2048]{2,1,0:T(8,128)} %vol_hbm.1, f32[4,32,2048]{2,1,0:T(8,128)} %meas.1, f32[2,2048]{1,0:T(2,128)} %constant.10.clone.line_hbm, bf16[2,3,512,512]{3,2,1,0:T(8,128)(2,1)} %constant.11.clone.fwd_big_hbm, ...), custom_call_target="tpu_custom_call" | custom-call | tf_op jit(solution)/shard_map/step/pallas_call | solution.py:540
  38.2 1.0 %copy.11 = f32[4,32,2048]{2,1,0:T(8,128)} copy(f32[4,32,2048]{2,1,0:T(8,128)S(1)} %step.1) | data formatting | bytes 2097152

commit v5 on v4

--- a/solution.py
+++ b/solution.py
@@ -505,7 +505,8 @@
             th, tl = inv_big[0, residue - 1], inv_big[1, residue - 1]
         else:
             th, tl = inv_small[0, residue // 4], inv_small[1, residue // 4]
-        spectral[:, at] = dot(high, th) + dot(low, th) + dot(high, tl)
+        both = dot(jnp.concatenate([high, low], 0), th)
+        spectral[:, at] = both[0:128] + both[128:256] + dot(high, tl)
 
     def part(first):
         return spectral[:, first : first + PART]

time: 39.3 us -> 39.2 us (level)
  no operation moved by 1% of the time
where the time goes in v5:
time: 39.2 us; the launch traced here: 39.1 us
  Pallas kernels  38.1 us (97%)
  local copies, waits for them, and re-layouts  0.97 us (2%)
    pallas_call x1, Pallas kernels, body(): pl.pallas_call(functools.partial(kernel, tiles), out_shape=pltpu.VMEM(vol...  38.1 us
    unnamed x1, local copies, waits for them, and re-layouts  0.97 us

profile of v5, /device:TPU:185, one launch (start us, length us, event | category | flops | bytes accessed | tf_op | source)
XLA Modules:
  0.0 39.1 jit_solution(16986164396868882843)
XLA Ops:
  0.0 38.1 %step.1 = f32[4,32,2048]{2,1,0:T(8,128)S(1)} custom-call(s32[4,64]{1,0:T(4,128)} %ray_hbm.1, s32[4,16]{1,0:T(4,128)} %defocus_hbm.1, f32[4,32,2048]{2,1,0:T(8,128)} %vol_hbm.1, f32[4,32,2048]{2,1,0:T(8,128)} %meas.1, f32[2,2048]{1,0:T(2,128)} %constant.10.clone.line_hbm, bf16[2,3,512,512]{3,2,1,0:T(8,128)(2,1)} %constant.11.clone.fwd_big_hbm, ...), custom_call_target="tpu_custom_call" | custom-call | tf_op jit(solution)/shard_map/step/pallas_call | solution.py:541
  38.1 1.0 %copy.11 = f32[4,32,2048]{2,1,0:T(8,128)} copy(f32[4,32,2048]{2,1,0:T(8,128)S(1)} %step.1) | data formatting | bytes 2097152
